TPU v7x, 768 devices: a whole 4x8x12 slice. The times are simulated.
768 devices in a mesh: node: 96 (over x, z, y_lo), local: 8 (over y_hi, core).
Axes of the slice: x: 4, y: 8 (y_hi: 4, y_lo: 2; y = y_hi * 2 + y_lo), z: 12, core: 2. Of those that a mesh axis runs over, the one named last changes fastest.
Arguments:
- tokens: bfloat16 [98304, 4096], P(('node', 'local')), may hold values from -6 to 6
- cotangent: bfloat16 [98304, 512], P(('node', 'local')), may hold values from -6 to 6
- codes: bfloat16 [8448, 256], P(('node', 'local')), may hold values from -6 to 6
- scales: bfloat16 [8448], P(('node', 'local')), may hold values from 0.0049743652 to 0.049804688
Outputs:
- keys: bfloat16 [98304, 512], P(('node', 'local'))
- grad_input: bfloat16 [98304, 4096], P(('node', 'local'))
- grad_weight: float32 [8448, 256], P(('node', 'local'))
All inputs are finite; a program needn't handle non-finite values.
Results may differ from a plain program's by a relative error of at most 0.015.
Values may be sent and summed in bfloat16 or wider, within the bound.
A program may use at most 64 MiB of HBM per device.

v0:
```python
import jax
import jax.numpy as jnp
from jax import lax
from jax.sharding import PartitionSpec as P


def per_device(tokens, cotangent, codes, scales):
    depth = tokens.shape[1]
    width = cotangent.shape[1]
    block_len = codes.shape[1]
    blocks = depth * width // block_len
    node_count = lax.axis_size("node")
    local_count = lax.axis_size("local")
    total_tokens = tokens.shape[0] * node_count * local_count
    factor = 1.0 / total_tokens**0.5
    got_codes, got_scales = (
        lax.all_gather(codes, ("node", "local"), axis=0, tiled=True),
        lax.all_gather(scales, ("node", "local"), axis=0, tiled=True),
    )
    weight = (
        (got_codes[:blocks].astype(jnp.float32) * got_scales[:blocks].astype(jnp.float32)[:, None])
        .astype(jnp.bfloat16)
        .reshape(depth, width)
    )
    keys = jnp.dot(tokens, weight, preferred_element_type=jnp.float32).astype(jnp.bfloat16)
    product = lax.dot_general(
        cotangent, weight, (((1,), (1,)), ((), ())), preferred_element_type=jnp.float32
    )
    grad_input = product.astype(jnp.bfloat16)
    term = (jnp.dot(tokens.T, cotangent, preferred_element_type=jnp.float32) * factor).astype(
        jnp.bfloat16
    )
    padded_rows = codes.shape[0] * node_count * local_count
    padded = jnp.pad(term.reshape(blocks, block_len), ((0, padded_rows - blocks), (0, 0)))
    grouped = padded.reshape(node_count, local_count, codes.shape[0], block_len)
    within = lax.psum_scatter(grouped, "local", scatter_dimension=1, tiled=True).astype(jnp.float32)
    across = lax.psum_scatter(within, "node", scatter_dimension=0, tiled=True)
    grad_weight = across.reshape(codes.shape[0], block_len)
    return (keys, grad_input, grad_weight)


def solution(mesh):
    in_specs = (
        P(("node", "local"), None),
        P(("node", "local"), None),
        P(("node", "local"), None),
        P(("node", "local")),
    )
    out_specs = (P(("node", "local"), None), P(("node", "local"), None), P(("node", "local"), None))
    return jax.shard_map(
        per_device, mesh=mesh, in_specs=in_specs, out_specs=out_specs, check_vma=False
    )
```

profile of v0, /device:TPU:48, one launch (start us, length us, event | category | flops | bytes accessed | tf_op | source)
XLA Modules:
  0.0 1755.2 jit_solution(7347622409765258789)
XLA Ops:
  8.0 0.0 copy-start
  8.0 0.0 all-gather.3.cloned.1.call-start
  8.1 0.7 all-gather.3.cloned.1.call-update
  8.7 0.0 reduce-scatter.3.cloned.1.call-start
  8.8 0.4 copy-done
  9.2 4.3 multiply_convert_fusion
  13.5 7.1 reshape.20
  20.6 3.7 pad.4
  24.3 8.4 reshape.21
  32.8 7.4 copy.14
  40.2 0.0 copy-start.2
  40.2 0.0 reduce-scatter.3.cloned.1.call-update
  40.2 1.3 dynamic-slice
  41.5 0.0 copy-done.2
  41.5 0.2 dynamic-update-slice
  41.7 117.9 %all-reduce.1 = bf16[8448]{0:T(1024)(128)(2,1)S(1)} all-reduce(bf16[8448]{0:T(1024)(128)(2,1)S(1)} %dynamic-update-slice), channel_id=1, replica_groups=mesh['node'=96,'local'=8] {'node','local'}, use_global_device_ids=true, to_apply=%add.1 | all-reduce | flops 8448 | bytes 33792
  159.6 1091.3 %all-gather.3.cloned.1.call-done = bf16[768,11,256]{2,1,0:T(8,128)(2,1)} async-done(((bf16[1,11,256]{2,1,0:T(8,128)(2,1)}), bf16[768,11,256]{2,1,0:T(8,128)(2,1)}) %all-gather.3.cloned.1.call-update) | async-done | bytes 4325392 | tf_op jit(solution)/shard_map/all_gather | solution.py:17
  1250.9 8.6 reshape.26
  1259.4 4.1 multiply_convert_fusion.1
  1263.6 0.0 copy-start.1
  1263.6 7.1 reshape.19
  1270.7 0.0 copy-done.1
  1270.7 3.4 fusion
  1274.2 1.3 copy.16
  1275.5 3.5 fusion.1
  1279.0 0.8 copy.15
  1279.7 0.0 reduce-scatter.3.cloned.1.call-done
  1279.7 466.7 %all-reduce.4 = f32[96,1,11,256]{3,0,2,1:T(8,128)S(1)} all-reduce(bf16[96,1,11,256]{3,0,2,1:T(8,128)(2,1)} %reduce-scatter.3.cloned.1.call-done), channel_id=3, replica_groups=mesh['node'=96,'local'=8] {'node'}, use_global_device_ids=true, to_apply=%region_1.2.clone | all-reduce | flops 270336 | bytes 1622016
  1746.5 0.7 constant_dynamic-slice_fusion
  1747.1 0.6 copy.21
  (2 shorter events, 0.0 us)
Async XLA Ops:
  8.0 1.2 copy-start
  8.0 1242.9 %all-gather.3.cloned.1.call-start = ((), (), s32[]{:S(2)}) async-start(), calls=%async_computation.2 | async-start | bytes 6299648 | tf_op jit(solution)/shard_map/all_gather | solution.py:17
  8.7 1271.0 %reduce-scatter.3.cloned.1.call-start = ((), (), s32[]{:S(2)}) async-start(), calls=%async_computation.1 | async-start | bytes 4866048 | tf_op jit(solution)/shard_map/reduce_scatter | solution.py:36
  40.2 1.3 copy-start.2
  1263.6 7.2 copy-start.1
Sparse Core Ops, SparseCore 0:
  11.4 1239.3 all-gather.2
Sparse Core Ops, SparseCore 1:
  40.3 69.5 reduce-scatter.2
where the time goes:
time: 1760 us
  waiting for transfers between devices  1090 us (62%)
  blocking collectives  585 us (33%)
  local copies, waits for them, and re-layouts  47.7 us (3%)
    all_gather x1, waiting for transfers between devices, per_device(): lax.all_gather(codes, ('node', 'local'), axis=0, tiled=True)  1090 us
    unnamed x2, blocking collectives  585 us
  transfers between devices with their start and end apart: 2, of which 1 were waited for; matrix products, arithmetic and copies ran while one was open for 3% of the time, Pallas kernels for 0%

commit v1 on v0

v1 whole, which is shorter than its diff:
```python
import functools

import jax
import jax.numpy as jnp
from jax import lax
from jax.experimental import pallas as pl
from jax.experimental.pallas import tpu as pltpu
from jax.sharding import PartitionSpec as P

NX, NY, NZ = 4, 8, 12
D, KV, T = 4096, 512, 128
HALF = KV // 2
OWN = 11
SLAB = OWN * NY
PLANE = SLAB * NZ
ROWS = PLANE * NX
CH = 512
NCH = D // CH
MESH = pl.DeviceIdType.MESH
F32, BF16 = jnp.float32, jnp.bfloat16


def mod(a, n):
    return lax.rem(a, n)


def kernel(
    factor,
    tok_hbm, cot_hbm, wx, keys, gi, gw,
    tok2, cot2, wpair, stage, ychunk, slab, xslab, zpack, zbuf, w32,
    part, xr, r32, frag, ysend, yrecv, ysum, zsend, zrecv, fin,
    gi32, gsend, grecv, ksend, krecv,
    lsem, sib_s, sib_r, ya_s, ya_r, xa_s, xa_r, za_s, za_r,
    xs_s, xs_r, ys_s, ys_r, zs_s, zs_r,
):
    node = lax.axis_index("node")
    local = lax.axis_index("local")
    x = lax.div(node, NZ * 2)
    z = mod(lax.div(node, 2), NZ)
    k = mod(node, 2) * 4 + lax.div(local, 2)
    c = mod(local, 2)

    def dev(x, z, k, c):
        return ((x * NZ + z) * 2 + lax.div(k, 4), mod(k, 4) * 2 + c)

    sib = dev(x, z, k, 1 - c)
    ydev = [dev(x, z, mod(k + o, NY), c) for o in range(1, NY)]
    xdev = [dev(mod(x + o, NX), z, k, c) for o in range(1, NX)]
    zdev = [dev(x, mod(z + o, NZ), k, c) for o in range(1, NZ)]

    def rc(src, dst, ss, rs, to):
        return pltpu.make_async_remote_copy(
            src_ref=src, dst_ref=dst, send_sem=ss, recv_sem=rs, device_id=to, device_id_type=MESH
        )

    load_tok = pltpu.make_async_copy(tok_hbm, tok2.at[0:T], lsem.at[0])
    load_cot = pltpu.make_async_copy(cot_hbm, cot2.at[0:T], lsem.at[1])
    load_tok.start()
    load_cot.start()

    barrier = pltpu.get_barrier_semaphore()
    partners = [sib] + zdev + ydev + xdev
    for to in partners:
        pl.semaphore_signal(barrier, inc=1, device_id=to, device_id_type=MESH)
    wpair[c] = wx[...]
    frag[...] = jnp.zeros_like(frag)
    ysum[...] = jnp.zeros_like(ysum)
    part[:, D:, :] = jnp.zeros((2, ROWS - D, 128), BF16)
    slab[...] = jnp.zeros_like(slab)
    stage[...] = jnp.zeros_like(stage)
    load_tok.wait()
    load_cot.wait()
    pl.semaphore_wait(barrier, len(partners))

    cw = rc(wpair.at[c], wpair.at[c], sib_s.at[0], sib_r.at[0], sib)
    cw.start()
    cc = rc(cot2.at[0:T], cot2.at[T : 2 * T], sib_s.at[1], sib_r.at[1], sib)
    cc.start()
    ct = rc(tok2.at[0:T], tok2.at[T : 2 * T], sib_s.at[2], sib_r.at[2], sib)
    ct.start()
    cw.wait()
    for r in range(OWN):
        rows = []
        for cc_ in range(2):
            i = 2 * r + cc_
            rows.append(wpair[i // OWN, i % OWN : i % OWN + 1, :])
        stage[r : r + 1, :] = jnp.where(c == 0, rows[0], rows[1])
    ychunk[k] = stage[...].astype(BF16)

    for o in range(1, NY):
        rc(ychunk.at[k], ychunk.at[k], ya_s.at[o - 1], ya_r.at[k], ydev[o - 1]).start()

    cc.wait()
    ct.wait()
    mine = pl.ds(pl.multiple_of(c * HALF, 128), HALF)

    def term_step(j, _):
        at = pl.multiple_of(j * CH, CH)
        a = tok2[:, pl.ds(at, CH)]
        t = lax.dot_general(a, cot2[:, mine], (((0,), (0,)), ((), ())), preferred_element_type=F32)
        t = (t * factor).astype(BF16)
        part[0, pl.ds(at, CH), :] = t[:, :128]
        part[1, pl.ds(at, CH), :] = t[:, 128:]
        return 0

    lax.fori_loop(0, NCH, term_step, 0)

    def plane(x):
        return pl.ds(pl.multiple_of(mod(x, NX) * PLANE, 16), PLANE)

    right, left = xdev[0], xdev[2]
    xsums = [
        rc(part.at[0, plane(x + 2)], xr.at[0], xs_s.at[0], xs_r.at[0], right),
        rc(part.at[1, plane(x + 2)], xr.at[1], xs_s.at[1], xs_r.at[1], left),
        rc(part.at[1, plane(x + 1)], xr.at[2], xs_s.at[2], xs_r.at[2], right),
        rc(part.at[0, plane(x + 3)], xr.at[3], xs_s.at[3], xs_r.at[3], left),
        rc(part.at[0, plane(x + 1)], xr.at[4], xs_s.at[4], xs_r.at[4], right),
        rc(part.at[1, plane(x + 3)], xr.at[5], xs_s.at[5], xs_r.at[5], left),
    ]
    for s in range(4):
        xsums[s].start()

    for o in range(1, NY):
        ks = mod(k + o, NY)
        rc(ychunk.at[ks], ychunk.at[ks], ya_s.at[o - 1], ya_r.at[ks], ydev[o - 1]).wait()
    for j in range(NY):
        slab[OWN * j : OWN * (j + 1), :] = ychunk[j].astype(F32)[:OWN]
    xslab[x] = slab[...].astype(BF16)
    for o in range(1, NX):
        rc(xslab.at[x], xslab.at[x], xa_s.at[o - 1], xa_r.at[x], xdev[o - 1]).start()
    for o in range(1, NX):
        xs = mod(x + o, NX)
        rc(xslab.at[xs], xslab.at[xs], xa_s.at[o - 1], xa_r.at[xs], xdev[o - 1]).wait()
    for q in range(2):
        zpack[0:SLAB, :] = xslab[2 * q].astype(F32)[:SLAB]
        zpack[SLAB : 2 * SLAB, :] = xslab[2 * q + 1].astype(F32)[:SLAB]
        zbuf[z, q] = zpack[...].astype(BF16)

    zright, zleft = zdev[0], zdev[NZ - 2]

    def zcopy(way, t, q):
        at = mod(z + (NZ - (t - 1) if way == 0 else t - 1), NZ)
        return rc(
            zbuf.at[at, q], zbuf.at[at, q], za_s.at[way, t - 1, q], za_r.at[at, q],
            zright if way == 0 else zleft,
        )

    def zarrived(way, t, q):
        at = mod(z + (NZ - t if way == 0 else t), NZ)
        rc(
            zbuf.at[at, q], zbuf.at[at, q], za_s.at[way, t - 1, q], za_r.at[at, q],
            zright if way == 0 else zleft,
        ).wait_recv()

    def zmoves(t):
        if t < 6:
            return [(0, 0), (1, 0), (0, 1), (1, 1)]
        return [(0, 0), (1, 1)]

    def place(at, q):
        v = zbuf[at, q].astype(F32)
        for e in range(2):
            to = pl.multiple_of((2 * q + e) * PLANE + at * SLAB, 8)
            w32[pl.ds(to, SLAB), :] = v[e * SLAB : (e + 1) * SLAB]

    def zstep(t):
        for way, q in zmoves(t):
            zarrived(way, t, q)
            if t < 6 and (way, q) in zmoves(t + 1):
                zcopy(way, t + 1, q).start()
        for way, q in zmoves(t):
            place(mod(z + (NZ - t if way == 0 else t), NZ), q)

    for way, q in zmoves(1):
        zcopy(way, 1, q).start()
    for q in range(2):
        place(z, q)
    zstep(1)

    def hand_on(s, h, p):
        xsums[s].wait_recv()
        start = mod(x + p, NX) * PLANE

        def add(j, _):
            rows = pl.ds(pl.multiple_of(start + j * 96, 16), 96)
            got = xr[s, pl.ds(pl.multiple_of(j * 96, 16), 96), :].astype(F32)
            part[h, rows, :] = (part[h, rows, :].astype(F32) + got).astype(BF16)
            return 0

        lax.fori_loop(0, PLANE // 96, add, 0)
        xsums[s + 4].start()

    hand_on(0, 0, 1)
    hand_on(1, 1, 3)
    zstep(2)
    zstep(3)
    for s in (2, 3, 4, 5):
        xsums[s].wait_recv()

    def root(j, _):
        at = pl.multiple_of(j * 96, 16)
        rows = pl.ds(at, 96)
        own = pl.ds(pl.multiple_of(x * PLANE + at, 16), 96)
        a = part[0, own, :].astype(F32) + xr[3, rows, :].astype(F32) + xr[4, rows, :].astype(F32)
        b = part[1, own, :].astype(F32) + xr[2, rows, :].astype(F32) + xr[5, rows, :].astype(F32)
        r32[rows, 0:128] = a
        r32[rows, 128:256] = b
        return 0

    lax.fori_loop(0, PLANE // 96, root, 0)

    def cut(zz, _):
        view = r32.at[pl.ds(pl.multiple_of(zz * 4 * SLAB, 8), 4 * SLAB)]
        for kk in range(NY):
            for i in range(4):
                at = SLAB * i + OWN * kk
                frag[kk, OWN * i : OWN * (i + 1), :] = view[at : at + OWN, :]
        for kk in range(NY):
            ysend[kk, zz] = frag[kk].astype(BF16)
        return 0

    lax.fori_loop(0, 3, cut, 0)
    for o in range(1, NY):
        kt = mod(k + o, NY)
        rc(ysend.at[kt], yrecv.at[k], ys_s.at[o - 1], ys_r.at[k], ydev[o - 1]).start()
    yrecv[k] = ysend[k]

    zstep(4)
    zstep(5)
    zstep(6)

    for o in range(1, NY):
        ks = mod(k + o, NY)
        rc(ysend.at[ks], yrecv.at[ks], ys_s.at[o - 1], ys_r.at[ks], ydev[o - 1]).wait()
    for zz in range(3):
        s = yrecv[0, zz].astype(F32)
        for kk in range(1, NY):
            s = s + yrecv[kk, zz].astype(F32)
        ysum[0:48, :] = s
        for i in range(4):
            zsend[4 * zz + i] = ysum[OWN * i : OWN * i + 16, :].astype(BF16)
    for o in range(1, NZ):
        zt = mod(z + o, NZ)
        rc(zsend.at[zt], zrecv.at[z], zs_s.at[o - 1], zs_r.at[z], zdev[o - 1]).start()
    zrecv[z] = zsend[z]

    def out_step(j, acc):
        at = pl.multiple_of(j * CH, CH)
        w = w32[pl.ds(at, CH), :].astype(BF16)
        acc = acc + jnp.dot(tok2[:, pl.ds(at, CH)], w, preferred_element_type=F32)
        g = lax.dot_general(cot2[:, mine], w, (((1,), (1,)), ((), ())), preferred_element_type=F32)
        gi32[j] = g[:T]
        gsend[j] = g[T:].astype(BF16)
        rc(gsend.at[j], grecv.at[j], sib_s.at[5 + j], sib_r.at[5 + j], sib).start()
        return acc

    acc = lax.fori_loop(0, NCH, out_step, jnp.zeros((2 * T, HALF), F32))
    other = pl.ds(pl.multiple_of((1 - c) * HALF, 128), HALF)
    keys[:, mine] = acc[:T].astype(BF16)
    ksend[...] = acc[T:].astype(BF16)
    ck = rc(ksend, krecv, sib_s.at[3], sib_r.at[3], sib)
    ck.start()

    def join(j, _):
        rc(gsend.at[j], grecv.at[j], sib_s.at[5 + j], sib_r.at[5 + j], sib).wait()
        at = pl.multiple_of(j * CH, CH)
        gi[:, pl.ds(at, CH)] = (gi32[j] + grecv[j].astype(F32)).astype(BF16)
        return 0

    lax.fori_loop(0, NCH, join, 0)
    ck.wait()
    keys[:, other] = krecv[...]

    for o in range(1, NZ):
        zs = mod(z + o, NZ)
        rc(zsend.at[zs], zrecv.at[zs], zs_s.at[o - 1], zs_r.at[zs], zdev[o - 1]).wait()
    s = zrecv[0].astype(F32)
    for j in range(1, NZ):
        s = s + zrecv[j].astype(F32)
    fin[c] = s
    cf = rc(fin.at[c], fin.at[c], sib_s.at[4], sib_r.at[4], sib)
    cf.start()

    for t in range(1, 7):
        for way, q in zmoves(t):
            zcopy(way, t, q).wait_send()
    for s in range(6):
        xsums[s].wait_send()
    cf.wait()
    for r in range(OWN):
        rows = []
        for cc_ in range(2):
            i = OWN * cc_ + r
            rows.append(fin[i % 2, i // 2 : i // 2 + 1, :])
        gw[r : r + 1, :] = jnp.where(c == 0, rows[0], rows[1])


def per_device(tokens, cotangent, codes, scales):
    total = tokens.shape[0] * lax.axis_size("node") * lax.axis_size("local")
    wx = codes.astype(F32) * scales.astype(F32)[:, None]
    wx = jnp.pad(wx, ((0, 16 - OWN), (0, 0)))
    dma = pltpu.SemaphoreType.DMA
    scratch = [
        pltpu.VMEM((2 * T, D), BF16),
        pltpu.VMEM((2 * T, KV), BF16),
        pltpu.VMEM((2, 16, HALF), F32),
        pltpu.VMEM((16, HALF), F32),
        pltpu.VMEM((NY, 16, HALF), BF16),
        pltpu.VMEM((96, HALF), F32),
        pltpu.VMEM((NX, 96, HALF), BF16),
        pltpu.VMEM((2 * SLAB, HALF), F32),
        pltpu.VMEM((NZ, 2, 2 * SLAB, HALF), BF16),
        pltpu.VMEM((ROWS, HALF), F32),
        pltpu.VMEM((2, ROWS, 128), BF16),
        pltpu.VMEM((6, PLANE, 128), BF16),
        pltpu.VMEM((PLANE, HALF), F32),
        pltpu.VMEM((NY, 48, HALF), F32),
        pltpu.VMEM((NY, 3, 48, HALF), BF16),
        pltpu.VMEM((NY, 3, 48, HALF), BF16),
        pltpu.VMEM((56, HALF), F32),
        pltpu.VMEM((NZ, 16, HALF), BF16),
        pltpu.VMEM((NZ, 16, HALF), BF16),
        pltpu.VMEM((2, 16, HALF), F32),
        pltpu.VMEM((NCH, T, CH), F32),
        pltpu.VMEM((NCH, T, CH), BF16),
        pltpu.VMEM((NCH, T, CH), BF16),
        pltpu.VMEM((T, HALF), BF16),
        pltpu.VMEM((T, HALF), BF16),
        dma((2,)),
        dma((5 + NCH,)), dma((5 + NCH,)),
        dma((NY - 1,)), dma((NY,)),
        dma((NX - 1,)), dma((NX,)),
        dma((2, 6, 2)), dma((NZ, 2)),
        dma((6,)), dma((6,)),
        dma((NY - 1,)), dma((NY,)),
        dma((NZ - 1,)), dma((NZ,)),
    ]
    vmem = pl.BlockSpec(memory_space=pltpu.VMEM)
    hbm = pl.BlockSpec(memory_space=pl.ANY)
    return pl.pallas_call(
        functools.partial(kernel, 1.0 / total**0.5),
        out_shape=(
            jax.ShapeDtypeStruct((T, KV), BF16),
            jax.ShapeDtypeStruct((T, D), BF16),
            jax.ShapeDtypeStruct((OWN, HALF), F32),
        ),
        in_specs=[hbm, hbm, vmem],
        out_specs=(vmem, vmem, vmem),
        scratch_shapes=scratch,
        compiler_params=pltpu.CompilerParams(
            collective_id=0, has_side_effects=True, vmem_limit_bytes=44 << 20
        ),
        name="fused",
    )(tokens, cotangent, wx)


def solution(mesh):
    in_specs = (
        P(("node", "local"), None),
        P(("node", "local"), None),
        P(("node", "local"), None),
        P(("node", "local")),
    )
    out_specs = (P(("node", "local"), None), P(("node", "local"), None), P(("node", "local"), None))
    return jax.shard_map(
        per_device, mesh=mesh, in_specs=in_specs, out_specs=out_specs, check_vma=False
    )
```

time: 1760 us -> 87.5 us (0.05)
  the two profiles are of different devices: /device:TPU:48 before, /device:TPU:1 now
where the time goes in v1:
time: 87.5 us; the launch traced here: 87.3 us
  Pallas kernels  80.9 us (92%)
  local copies, waits for them, and re-layouts  4.37 us (5%)
  other arithmetic  1.43 us (2%)
    pallas_call x1, Pallas kernels, per_device(): pl.pallas_call(functools.partial(kernel, 1.0 / total ** 0.5), out_shape=(...  80.9 us
    unnamed x7, local copies, waits for them, and re-layouts  4.36 us

profile of v1, /device:TPU:1, one launch (start us, length us, event | category | flops | bytes accessed | tf_op | source)
XLA Modules:
  0.0 87.3 jit_solution(12036557070788995933)
XLA Ops:
  0.6 0.7 convert_element_type.9
  1.3 0.8 convert_multiply_fusion
  2.1 0.0 copy-start
  2.1 1.2 %copy-done = bf16[128,4096]{1,0:T(8,128)(2,1)S(1)} copy-done((bf16[128,4096]{1,0:T(8,128)(2,1)S(1)}, bf16[128,4096]{1,0:T(8,128)(2,1)}, u32[]{:S(2)}) %copy-start) | copy-done | bytes 1048600
  3.3 0.0 copy-start.1
  3.3 0.9 %copy-done.1 = bf16[128,512]{1,0:T(8,128)(2,1)S(1)} copy-done((bf16[128,512]{1,0:T(8,128)(2,1)S(1)}, bf16[128,512]{1,0:T(8,128)(2,1)}, u32[]{:S(2)}) %copy-start.1) | copy-done | bytes 131096
  4.2 80.9 %fused.1 = (bf16[128,512]{1,0:T(8,128)(2,1)S(1)}, bf16[128,4096]{1,0:T(8,128)(2,1)S(1)}, f32[11,256]{1,0:T(8,128)S(1)}) custom-call(bf16[128,4096]{1,0:T(8,128)(2,1)S(1)} %copy-done, bf16[128,512]{1,0:T(8,128)(2,1)S(1)} %copy-done.1, f32[16,256]{1,0:T(8,128)S(1)} %pad.4.wx), custom_call_target="tpu_custom_call" | custom-call | tf_op jit(solution)/shard_map/fused/pallas_call | solution.py:340
  85.1 0.7 copy.10
  85.7 1.0 %copy.11 = bf16[128,4096]{1,0:T(8,128)(2,1)} copy(bf16[128,4096]{1,0:T(8,128)(2,1)S(1)} %get-tuple-element.7) | data formatting | bytes 2097152
  86.7 0.6 copy.12
  (1 shorter events, 0.0 us)
Async XLA Ops:
  2.1 1.2 %copy-start = (bf16[128,4096]{1,0:T(8,128)(2,1)S(1)}, bf16[128,4096]{1,0:T(8,128)(2,1)}, u32[]{:S(2)}) copy-start(bf16[128,4096]{1,0:T(8,128)(2,1)} %tok_hbm.1) | copy-start | bytes 3145732
  3.3 0.9 %copy-start.1 = (bf16[128,512]{1,0:T(8,128)(2,1)S(1)}, bf16[128,512]{1,0:T(8,128)(2,1)}, u32[]{:S(2)}) copy-start(bf16[128,512]{1,0:T(8,128)(2,1)} %cot_hbm.1) | copy-start | bytes 393220

commit v2 on v1

v2 whole, which is shorter than its diff:
```python
import functools

import jax
import jax.numpy as jnp
from jax import lax
from jax.experimental import pallas as pl
from jax.experimental.pallas import tpu as pltpu
from jax.sharding import PartitionSpec as P

NX, NY, NZ = 4, 8, 12
D, KV, T = 4096, 512, 128
HALF = KV // 2
OWN = 11
SLAB = OWN * NY
PLANE = SLAB * NZ
ROWS = PLANE * NX
PAD = ROWS - D
PIECE = 4 * SLAB
CH = 512
NCH = D // CH
MESH = pl.DeviceIdType.MESH
F32, BF16 = jnp.float32, jnp.bfloat16


def mod(a, n):
    return lax.rem(a, n)


def kernel(
    factor,
    tok_hbm, cot_hbm, codes_hbm, scales_hbm, keys, gi, gw,
    tok2, cot2, wpair, stage, ychunk, slab, xslab, zpack, zbuf, w32,
    part, xr, r32, frag, ysend, yrecv, ysum, zsend, zrecv, fin,
    gi32, gsend, grecv, ksend, krecv, codes, scales,
    lsem, sib_s, sib_r, ya_s, ya_r, xa_s, xa_r, za_s, za_r, zy_s, zy_r,
    xs_s, xs_r, ys_s, ys_r, zs_s, zs_r,
):
    node = lax.axis_index("node")
    local = lax.axis_index("local")
    x = lax.div(node, NZ * 2)
    z = mod(lax.div(node, 2), NZ)
    k = mod(node, 2) * 4 + lax.div(local, 2)
    y = lax.div(local, 2) * 2 + mod(node, 2)
    c = mod(local, 2)
    odd = mod(node, 2)

    def dev(x, z, k, c):
        return ((x * NZ + z) * 2 + lax.div(k, 4), mod(k, 4) * 2 + c)

    def at_y(y):
        y = mod(y, NY)
        return dev(x, z, mod(y, 2) * 4 + lax.div(y, 2), c)

    sib = dev(x, z, k, 1 - c)
    ydev = [dev(x, z, mod(k + o, NY), c) for o in range(1, NY)]
    xdev = [dev(mod(x + o, NX), z, k, c) for o in range(1, NX)]
    zdev = [dev(x, mod(z + o, NZ), k, c) for o in range(1, NZ)]
    right, left = xdev[0], xdev[2]
    zright, zleft = zdev[0], zdev[NZ - 2]
    up, down = at_y(y + 1), at_y(y + NY - 1)

    def rc(src, dst, ss, rs, to):
        return pltpu.make_async_remote_copy(
            src_ref=src, dst_ref=dst, send_sem=ss, recv_sem=rs, device_id=to, device_id_type=MESH
        )

    barrier = pltpu.get_barrier_semaphore()
    partners = [sib] + zdev + ydev + xdev
    for to in partners:
        pl.semaphore_signal(barrier, inc=1, device_id=to, device_id_type=MESH)
    load_cot = pltpu.make_async_copy(cot_hbm, cot2.at[0:T], lsem.at[1])
    load_tok = pltpu.make_async_copy(tok_hbm, tok2.at[0:T, 0:D], lsem.at[0])
    load_codes = pltpu.make_async_copy(codes_hbm, codes, lsem.at[2])
    load_scales = pltpu.make_async_copy(scales_hbm, scales, lsem.at[3])
    for load in (load_scales, load_codes, load_cot, load_tok):
        load.start()
    frag[...] = jnp.zeros_like(frag)
    ysum[...] = jnp.zeros_like(ysum)
    tok2[:, D:] = jnp.zeros((2 * T, PAD), BF16)
    slab[...] = jnp.zeros_like(slab)
    stage[...] = jnp.zeros_like(stage)
    load_scales.wait()
    load_codes.wait()
    eye = lax.broadcasted_iota(jnp.int32, (OWN, OWN), 0) == lax.broadcasted_iota(
        jnp.int32, (OWN, OWN), 1
    )
    row = jnp.broadcast_to(scales[...].astype(F32), (OWN, OWN))
    column = jnp.sum(jnp.where(eye, row, 0.0), axis=1, keepdims=True)
    wpair[c, 0:OWN, :] = codes[...].astype(F32) * column
    load_cot.wait()
    load_tok.wait()
    pl.semaphore_wait(barrier, len(partners))

    cw = rc(wpair.at[c], wpair.at[c], sib_s.at[0], sib_r.at[0], sib)
    cw.start()
    cc = rc(cot2.at[0:T], cot2.at[T : 2 * T], sib_s.at[1], sib_r.at[1], sib)
    cc.start()
    ct = rc(tok2.at[0:T, 0:D], tok2.at[T : 2 * T, 0:D], sib_s.at[2], sib_r.at[2], sib)
    ct.start()
    cw.wait()
    for r in range(OWN):
        rows = []
        for e in range(2):
            i = 2 * r + e
            rows.append(wpair[i // OWN, i % OWN : i % OWN + 1, :])
        stage[r : r + 1, :] = jnp.where(c == 0, rows[0], rows[1])
    ychunk[k] = stage[...].astype(BF16)

    for o in range(1, NY):
        rc(ychunk.at[k], ychunk.at[k], ya_s.at[o - 1], ya_r.at[k], ydev[o - 1]).start()

    cc.wait()
    ct.wait()
    mine = pl.ds(pl.multiple_of(c * HALF, 128), HALF)

    def term(p):
        def step(j, _):
            at = pl.multiple_of(p * 1024 + j * 384, 128)
            t = lax.dot_general(
                tok2[:, pl.ds(at, 384)], cot2[:, mine], (((0,), (0,)), ((), ())),
                preferred_element_type=F32,
            )
            t = (t * factor).astype(BF16)
            to = pl.ds(pl.multiple_of(j * 384, 16), 384)
            part[p, 0, to, :] = t[:, :128]
            part[p, 1, to, :] = t[:, 128:]
            return 0

        lax.fori_loop(0, 3, step, 0)

    def piece(p, zz):
        return pl.ds(pl.multiple_of(p * 32 + zz * PIECE, 16), PIECE)

    pr, pf, pl_ = mod(x + 1, NX), mod(x + 2, NX), mod(x + 3, NX)

    def xsum(s, zz):
        p, h, to = [
            (pf, 0, right), (pf, 1, left), (pr, 1, right), (pl_, 0, left), (pr, 0, right), (pl_, 1, left),
        ][s]
        return rc(
            part.at[p, h, piece(p, zz)], xr.at[s, zz], xs_s.at[s, zz], xs_r.at[s, zz], to
        )

    def far(zz):
        xsum(0, zz).start()
        xsum(1, zz).start()

    def near(zz):
        xsum(2, zz).start()
        xsum(3, zz).start()

    def hand_on(zz):
        for s, h, p in ((0, 0, pr), (1, 1, pl_)):
            xsum(s, zz).wait_recv()
            rows = piece(p, zz)
            part[p, h, rows, :] = (
                part[p, h, rows, :].astype(F32) + xr[s, zz].astype(F32)
            ).astype(BF16)
            xsum(s + 4, zz).start()

    def root(zz):
        for s in (2, 3, 4, 5):
            xsum(s, zz).wait_recv()
        own = piece(x, zz)
        r32[:, 0:128] = part[x, 0, own, :].astype(F32) + (
            xr[3, zz].astype(F32) + xr[4, zz].astype(F32)
        )
        r32[:, 128:256] = part[x, 1, own, :].astype(F32) + (
            xr[2, zz].astype(F32) + xr[5, zz].astype(F32)
        )
        for kk in range(NY):
            for i in range(4):
                at = SLAB * i + OWN * kk
                frag[kk, OWN * i : OWN * (i + 1), :] = r32[at : at + OWN, :]
        for kk in range(NY):
            ysend[zz, kk] = frag[kk].astype(BF16)
        for o in range(1, NY):
            kt = mod(k + o, NY)
            rc(
                ysend.at[zz, kt], yrecv.at[zz, k], ys_s.at[zz, o - 1], ys_r.at[zz, k], ydev[o - 1]
            ).start()
        yrecv[zz, k] = ysend[zz, k]

    def zsum(zz):
        for o in range(1, NY):
            ks = mod(k + o, NY)
            rc(
                ysend.at[zz, ks], yrecv.at[zz, ks], ys_s.at[zz, o - 1], ys_r.at[zz, ks], ydev[o - 1]
            ).wait()
        s = yrecv[zz, 0].astype(F32)
        for kk in range(1, NY):
            s = s + yrecv[zz, kk].astype(F32)
        ysum[0:48, :] = s
        for i in range(4):
            zt = 4 * zz + i
            zsend[zt] = ysum[OWN * i : OWN * i + 16, :].astype(BF16)

            @pl.when(zt != z)
            def _():
                rc(zsend.at[zt], zrecv.at[z], zs_s.at[zt], zs_r.at[z], dev(x, zt, k, c)).start()

            @pl.when(zt == z)
            def _():
                zrecv[zt] = zsend[zt]

    term(pf)
    far(0)
    term(pr)
    term(pl_)
    near(0)
    term(x)

    for o in range(1, NY):
        ks = mod(k + o, NY)
        rc(ychunk.at[ks], ychunk.at[ks], ya_s.at[o - 1], ya_r.at[ks], ydev[o - 1]).wait()
    for j in range(NY):
        slab[OWN * j : OWN * (j + 1), :] = ychunk[j].astype(F32)[:OWN]
    xslab[x] = slab[...].astype(BF16)
    for o in range(1, NX):
        rc(xslab.at[x], xslab.at[x], xa_s.at[o - 1], xa_r.at[x], xdev[o - 1]).start()
    far(1)
    hand_on(0)
    near(1)
    far(2)
    for o in range(1, NX):
        xs = mod(x + o, NX)
        rc(xslab.at[xs], xslab.at[xs], xa_s.at[o - 1], xa_r.at[xs], xdev[o - 1]).wait()
    for q in range(2):
        zpack[0:SLAB, :] = xslab[2 * q].astype(F32)[:SLAB]
        zpack[SLAB : 2 * SLAB, :] = xslab[2 * q + 1].astype(F32)[:SLAB]
        for h in range(2):
            zbuf[z, q, h] = zpack[:, 128 * h : 128 * h + 128].astype(BF16)

    def zslot(way, t):
        return mod(z + (NZ - t if way == 0 else t), NZ)

    def zhalves(way, t):
        return (0, 1) if t < 6 else (way,)

    def zcopy(way, t, h):
        at = zslot(way, t - 1)
        return rc(
            zbuf.at[at, odd, h], zbuf.at[at, odd, h], za_s.at[way, t - 1, h], za_r.at[at, h],
            zright if way == 0 else zleft,
        )

    def zarrived(way, t, h):
        at = zslot(way, t)
        rc(
            zbuf.at[at, odd, h], zbuf.at[at, odd, h], za_s.at[way, t - 1, h], za_r.at[at, h],
            zright if way == 0 else zleft,
        ).wait_recv()

    def across(way, t, h, q):
        at = zslot(way, t)
        return rc(
            zbuf.at[at, q, h], zbuf.at[at, q, h], zy_s.at[at, h], zy_r.at[at, h],
            up if h == 0 else down,
        )

    def place(at, q, h):
        v = zbuf[at, q, h].astype(F32)
        for e in range(2):
            to = pl.multiple_of((2 * q + e) * PLANE + at * SLAB, 8)
            w32[pl.ds(to, SLAB), 128 * h : 128 * h + 128] = v[e * SLAB : (e + 1) * SLAB]

    def zstep(t):
        for h in range(2):
            for way in range(2):
                if h not in zhalves(way, t):
                    continue
                zarrived(way, t, h)
                if t < 6 and h in zhalves(way, t + 1):
                    zcopy(way, t + 1, h).start()
                across(way, t, h, odd).start()
        for h in range(2):
            for way in range(2):
                if h in zhalves(way, t):
                    place(zslot(way, t), odd, h)

    def from_y(t):
        for h in range(2):
            for way in range(2):
                if h in zhalves(way, t):
                    across(way, t, h, 1 - odd).wait_recv()
                    place(zslot(way, t), 1 - odd, h)

    for h in range(2):
        for way in range(2):
            zcopy(way, 1, h).start()
    for q in range(2):
        for h in range(2):
            place(z, q, h)
    hand_on(1)
    near(2)
    zstep(1)
    root(0)
    zstep(2)
    hand_on(2)
    zstep(3)
    from_y(1)
    root(1)
    zstep(4)
    from_y(2)
    zsum(0)
    zstep(5)
    from_y(3)
    root(2)
    zstep(6)
    from_y(4)
    zsum(1)
    from_y(5)
    from_y(6)
    zsum(2)

    def out_step(j, acc):
        at = pl.multiple_of(j * CH, CH)
        w = w32[pl.ds(at, CH), :].astype(BF16)
        acc = acc + jnp.dot(tok2[:, pl.ds(at, CH)], w, preferred_element_type=F32)
        g = lax.dot_general(cot2[:, mine], w, (((1,), (1,)), ((), ())), preferred_element_type=F32)
        gi32[j] = g[:T]
        gsend[j] = g[T:].astype(BF16)
        rc(gsend.at[j], grecv.at[j], sib_s.at[5 + j], sib_r.at[5 + j], sib).start()
        return acc

    acc = lax.fori_loop(0, NCH, out_step, jnp.zeros((2 * T, HALF), F32))
    other = pl.ds(pl.multiple_of((1 - c) * HALF, 128), HALF)
    keys[:, mine] = acc[:T].astype(BF16)
    ksend[...] = acc[T:].astype(BF16)
    ck = rc(ksend, krecv, sib_s.at[3], sib_r.at[3], sib)
    ck.start()

    def join(j, _):
        rc(gsend.at[j], grecv.at[j], sib_s.at[5 + j], sib_r.at[5 + j], sib).wait()
        at = pl.multiple_of(j * CH, CH)
        gi[:, pl.ds(at, CH)] = (gi32[j] + grecv[j].astype(F32)).astype(BF16)
        return 0

    lax.fori_loop(0, NCH, join, 0)
    ck.wait()
    keys[:, other] = krecv[...]

    for o in range(1, NZ):
        zs = mod(z + o, NZ)
        rc(zsend.at[zs], zrecv.at[zs], zs_s.at[zs], zs_r.at[zs], zdev[o - 1]).wait()
    s = zrecv[0].astype(F32)
    for j in range(1, NZ):
        s = s + zrecv[j].astype(F32)
    fin[c] = s
    cf = rc(fin.at[c], fin.at[c], sib_s.at[4], sib_r.at[4], sib)
    cf.start()

    for t in range(1, 7):
        for way in range(2):
            for h in zhalves(way, t):
                zcopy(way, t, h).wait_send()
                across(way, t, h, odd).wait_send()
    for s in range(6):
        for zz in range(3):
            xsum(s, zz).wait_send()
    cf.wait()
    for r in range(OWN):
        rows = []
        for e in range(2):
            i = OWN * e + r
            rows.append(fin[i % 2, i // 2 : i // 2 + 1, :])
        gw[r : r + 1, :] = jnp.where(c == 0, rows[0], rows[1])


def store(keys, gi, gw, keys_out, gi_out, gw_out, sem):
    copies = [
        pltpu.make_async_copy(gi, gi_out, sem.at[0]),
        pltpu.make_async_copy(keys, keys_out, sem.at[1]),
        pltpu.make_async_copy(gw, gw_out, sem.at[2]),
    ]
    for copy in copies:
        copy.start()
    for copy in copies:
        copy.wait()


def per_device(tokens, cotangent, codes, scales):
    total = tokens.shape[0] * lax.axis_size("node") * lax.axis_size("local")
    dma = pltpu.SemaphoreType.DMA
    scratch = [
        pltpu.VMEM((2 * T, ROWS), BF16),
        pltpu.VMEM((2 * T, KV), BF16),
        pltpu.VMEM((2, 16, HALF), F32),
        pltpu.VMEM((16, HALF), F32),
        pltpu.VMEM((NY, 16, HALF), BF16),
        pltpu.VMEM((96, HALF), F32),
        pltpu.VMEM((NX, 96, HALF), BF16),
        pltpu.VMEM((2 * SLAB, HALF), F32),
        pltpu.VMEM((NZ, 2, 2, 2 * SLAB, 128), BF16),
        pltpu.VMEM((ROWS, HALF), F32),
        pltpu.VMEM((NX, 2, 1152, 128), BF16),
        pltpu.VMEM((6, 3, PIECE, 128), BF16),
        pltpu.VMEM((PIECE, HALF), F32),
        pltpu.VMEM((NY, 48, HALF), F32),
        pltpu.VMEM((3, NY, 48, HALF), BF16),
        pltpu.VMEM((3, NY, 48, HALF), BF16),
        pltpu.VMEM((56, HALF), F32),
        pltpu.VMEM((NZ, 16, HALF), BF16),
        pltpu.VMEM((NZ, 16, HALF), BF16),
        pltpu.VMEM((2, 16, HALF), F32),
        pltpu.VMEM((NCH, T, CH), F32),
        pltpu.VMEM((NCH, T, CH), BF16),
        pltpu.VMEM((NCH, T, CH), BF16),
        pltpu.VMEM((T, HALF), BF16),
        pltpu.VMEM((T, HALF), BF16),
        pltpu.VMEM((OWN, HALF), BF16),
        pltpu.VMEM((1, OWN), BF16),
        dma((4,)),
        dma((5 + NCH,)), dma((5 + NCH,)),
        dma((NY - 1,)), dma((NY,)),
        dma((NX - 1,)), dma((NX,)),
        dma((2, 6, 2)), dma((NZ, 2)), dma((NZ, 2)), dma((NZ, 2)),
        dma((6, 3)), dma((6, 3)),
        dma((3, NY - 1)), dma((3, NY)),
        dma((NZ,)), dma((NZ,)),
    ]
    vmem = pl.BlockSpec(memory_space=pltpu.VMEM)
    hbm = pl.BlockSpec(memory_space=pl.ANY)
    arrays = (tokens, cotangent, codes, scales.reshape(1, OWN))
    keys, gi, gw = pl.pallas_call(
        functools.partial(kernel, 1.0 / total**0.5),
        out_shape=(
            jax.ShapeDtypeStruct((T, KV), BF16),
            jax.ShapeDtypeStruct((T, D), BF16),
            jax.ShapeDtypeStruct((OWN, HALF), F32),
        ),
        in_specs=[hbm] * 4,
        out_specs=(vmem, vmem, vmem),
        scratch_shapes=scratch,
        compiler_params=pltpu.CompilerParams(
            collective_id=0, has_side_effects=True, vmem_limit_bytes=40 << 20
        ),
        name="fused",
    )(*[pltpu.with_memory_space_constraint(a, pltpu.HBM) for a in arrays])
    return pl.pallas_call(
        store,
        out_shape=(
            jax.ShapeDtypeStruct((T, KV), BF16),
            jax.ShapeDtypeStruct((T, D), BF16),
            jax.ShapeDtypeStruct((OWN, HALF), F32),
        ),
        in_specs=[vmem, vmem, vmem],
        out_specs=(hbm, hbm, hbm),
        scratch_shapes=[dma((3,))],
        name="store",
    )(*[pltpu.with_memory_space_constraint(a, pltpu.VMEM) for a in (keys, gi, gw)])


def solution(mesh):
    in_specs = (
        P(("node", "local"), None),
        P(("node", "local"), None),
        P(("node", "local"), None),
        P(("node", "local")),
    )
    out_specs = (P(("node", "local"), None), P(("node", "local"), None), P(("node", "local"), None))
    return jax.shard_map(
        per_device, mesh=mesh, in_specs=in_specs, out_specs=out_specs, check_vma=False
    )
```

time: 87.5 us -> 69.7 us (0.80)
  Pallas kernels: 80.9 us -> 68.9 us
  local copies, waits for them, and re-layouts: 4.37 us -> 0 us
  other arithmetic: 1.43 us -> 0 us
    pallas_call x1, Pallas kernels: 80.9 us -> 67.9 us  [per_device(): pl.pallas_call(functools.partial(kernel, 1.0 / total ** 0.5), out_shape=(...]
    unnamed x7 -> x0, local copies, waits for them, and re-layouts: 4.36 us -> none
    pallas_call x0 -> x1, Pallas kernels: none -> 1.03 us  [per_device(): pl.pallas_call(store, out_shape=(jax.ShapeDtypeStruct((T, KV), BF16), jax...]
where the time goes in v2:
time: 69.7 us; the launch traced here: 69.6 us
  Pallas kernels  68.9 us (99%)
    pallas_call x1, Pallas kernels, per_device(): pl.pallas_call(functools.partial(kernel, 1.0 / total ** 0.5), out_shape=(...  67.9 us

profile of v2, /device:TPU:1, one launch (start us, length us, event | category | flops | bytes accessed | tf_op | source)
XLA Modules:
  0.0 69.6 jit_solution(3591912212595507829)
XLA Ops:
  0.6 67.9 %fused.1 = (bf16[128,512]{1,0:T(8,128)(2,1)S(1)}, bf16[128,4096]{1,0:T(8,128)(2,1)S(1)}, f32[11,256]{1,0:T(8,128)S(1)}) custom-call(bf16[128,4096]{1,0:T(8,128)(2,1)} %tok_hbm.1, bf16[128,512]{1,0:T(8,128)(2,1)} %cot_hbm.1, bf16[11,256]{1,0:T(8,128)(2,1)} %codes_hbm.1, bf16[1,11]{1,0:T(2,128)(2,1)} %bitcast.1), custom_call_target="tpu_custom_call" | custom-call | tf_op jit(solution)/shard_map/fused/pallas_call | solution.py:425
  68.5 1.0 %store.1 = (bf16[128,512]{1,0:T(8,128)(2,1)}, bf16[128,4096]{1,0:T(8,128)(2,1)}, f32[11,256]{1,0:T(8,128)}) custom-call(bf16[128,512]{1,0:T(8,128)(2,1)S(1)} %get-tuple-element.6.keys, bf16[128,4096]{1,0:T(8,128)(2,1)S(1)} %get-tuple-element.7.gi, f32[11,256]{1,0:T(8,128)S(1)} %get-tuple-element.8.gw), custom_call_target="tpu_custom_call" | custom-call | tf_op jit(solution)/shard_map/store/pallas_call | solution.py:440

commit v3 on v2

--- a/solution.py
+++ b/solution.py
@@ -29,11 +29,10 @@
 def kernel(
     factor,
     tok_hbm, cot_hbm, codes_hbm, scales_hbm, keys, gi, gw,
-    tok2, cot2, wpair, stage, ychunk, slab, xslab, zpack, zbuf, w32,
-    part, xr, r32, frag, ysend, yrecv, ysum, zsend, zrecv, fin,
+    tok2, cot2, wpair, stage, chunk, zpack, zbuf, w32,
+    part, xr, r32, frag, ysend, ymid, yhalf, yrecv, ysum, zsend, zrecv, fin,
     gi32, gsend, grecv, ksend, krecv, codes, scales,
-    lsem, sib_s, sib_r, ya_s, ya_r, xa_s, xa_r, za_s, za_r, zy_s, zy_r,
-    xs_s, xs_r, ys_s, ys_r, zs_s, zs_r,
+    lsem, sib_s, sib_r, out, into, tk_r, za_r, zy_r, xs_r, ys_r,
 ):
     node = lax.axis_index("node")
     local = lax.axis_index("local")
@@ -42,7 +41,7 @@
     k = mod(node, 2) * 4 + lax.div(local, 2)
     y = lax.div(local, 2) * 2 + mod(node, 2)
     c = mod(local, 2)
-    odd = mod(node, 2)
+    odd = mod(x + node, 2)
 
     def dev(x, z, k, c):
         return ((x * NZ + z) * 2 + lax.div(k, 4), mod(k, 4) * 2 + c)
@@ -51,8 +50,11 @@
         y = mod(y, NY)
         return dev(x, z, mod(y, 2) * 4 + lax.div(y, 2), c)
 
+    def kof(d):
+        to = mod(y + NY + d, NY)
+        return mod(to, 2) * 4 + lax.div(to, 2)
+
     sib = dev(x, z, k, 1 - c)
-    ydev = [dev(x, z, mod(k + o, NY), c) for o in range(1, NY)]
     xdev = [dev(mod(x + o, NX), z, k, c) for o in range(1, NX)]
     zdev = [dev(x, mod(z + o, NZ), k, c) for o in range(1, NZ)]
     right, left = xdev[0], xdev[2]
@@ -64,20 +66,41 @@
             src_ref=src, dst_ref=dst, send_sem=ss, recv_sem=rs, device_id=to, device_id_type=MESH
         )
 
-    barrier = pltpu.get_barrier_semaphore()
-    partners = [sib] + zdev + ydev + xdev
-    for to in partners:
-        pl.semaphore_signal(barrier, inc=1, device_id=to, device_id_type=MESH)
+    def all_sent(stage, ref):
+        rc(ref, ref, out.at[stage], into.at[0], sib).wait_send()
+
+    def all_here(sem, ref):
+        rc(ref, ref, out.at[0], sem, sib).wait_recv()
+
+    def plane_dev(o):
+        return dev(mod(x + lax.div(o, NY), NX), z, mod(k + o, NY), c)
+
     load_cot = pltpu.make_async_copy(cot_hbm, cot2.at[0:T], lsem.at[1])
     load_tok = pltpu.make_async_copy(tok_hbm, tok2.at[0:T, 0:D], lsem.at[0])
     load_codes = pltpu.make_async_copy(codes_hbm, codes, lsem.at[2])
     load_scales = pltpu.make_async_copy(scales_hbm, scales, lsem.at[3])
     for load in (load_scales, load_codes, load_cot, load_tok):
         load.start()
+
+    barrier = pltpu.get_barrier_semaphore()
+
+    def signal(to):
+        pl.semaphore_signal(barrier, inc=1, device_id=to, device_id_type=MESH)
+
+    def signal_plane(o, _):
+        signal(plane_dev(o))
+        return 0
+
+    def signal_z(o, _):
+        signal(dev(x, mod(z + o, NZ), k, c))
+        return 0
+
+    signal(sib)
+    lax.fori_loop(1, NX * NY, signal_plane, 0)
+    lax.fori_loop(1, NZ, signal_z, 0)
     frag[...] = jnp.zeros_like(frag)
     ysum[...] = jnp.zeros_like(ysum)
     tok2[:, D:] = jnp.zeros((2 * T, PAD), BF16)
-    slab[...] = jnp.zeros_like(slab)
     stage[...] = jnp.zeros_like(stage)
     load_scales.wait()
     load_codes.wait()
@@ -87,16 +110,21 @@
     row = jnp.broadcast_to(scales[...].astype(F32), (OWN, OWN))
     column = jnp.sum(jnp.where(eye, row, 0.0), axis=1, keepdims=True)
     wpair[c, 0:OWN, :] = codes[...].astype(F32) * column
-    load_cot.wait()
-    load_tok.wait()
-    pl.semaphore_wait(barrier, len(partners))
+    pl.semaphore_wait(barrier, 1 + NX * NY - 1 + NZ - 1)
 
     cw = rc(wpair.at[c], wpair.at[c], sib_s.at[0], sib_r.at[0], sib)
     cw.start()
-    cc = rc(cot2.at[0:T], cot2.at[T : 2 * T], sib_s.at[1], sib_r.at[1], sib)
+    cc = rc(cot_hbm, cot2.at[T : 2 * T], sib_s.at[1], sib_r.at[1], sib)
     cc.start()
-    ct = rc(tok2.at[0:T, 0:D], tok2.at[T : 2 * T, 0:D], sib_s.at[2], sib_r.at[2], sib)
-    ct.start()
+
+    def quarter(o):
+        at = pl.ds(pl.multiple_of(mod(x + o, NX) * 1024, 1024), 1024)
+        return rc(
+            tok_hbm.at[:, at], tok2.at[T : 2 * T, at], out.at[0], tk_r.at[mod(x + o, NX)], sib
+        )
+
+    for o in (2, 3, 0, 1):
+        quarter(o).start()
     cw.wait()
     for r in range(OWN):
         rows = []
@@ -104,13 +132,21 @@
             i = 2 * r + e
             rows.append(wpair[i // OWN, i % OWN : i % OWN + 1, :])
         stage[r : r + 1, :] = jnp.where(c == 0, rows[0], rows[1])
-    ychunk[k] = stage[...].astype(BF16)
-
-    for o in range(1, NY):
-        rc(ychunk.at[k], ychunk.at[k], ya_s.at[o - 1], ya_r.at[k], ydev[o - 1]).start()
-
+    me = x * NY + k
+    chunk[me] = stage[...].astype(BF16)
+
+    def chunk_copy(o, slot):
+        return rc(chunk.at[slot], chunk.at[slot], out.at[1], into.at[0], plane_dev(o))
+
+    def chunk_start(i, _):
+        chunk_copy(NX * NY - 1 - i, me).start()
+        return 0
+
+    lax.fori_loop(0, NX * NY - 1, chunk_start, 0)
+
+    load_cot.wait()
+    load_tok.wait()
     cc.wait()
-    ct.wait()
     mine = pl.ds(pl.multiple_of(c * HALF, 128), HALF)
 
     def term(p):
@@ -138,7 +174,7 @@
             (pf, 0, right), (pf, 1, left), (pr, 1, right), (pl_, 0, left), (pr, 0, right), (pl_, 1, left),
         ][s]
         return rc(
-            part.at[p, h, piece(p, zz)], xr.at[s, zz], xs_s.at[s, zz], xs_r.at[s, zz], to
+            part.at[p, h, piece(p, zz)], xr.at[s, zz], out.at[4], xs_r.at[0 if s < 2 else 1, zz], to
         )
 
     def far(zz):
@@ -150,8 +186,8 @@
         xsum(3, zz).start()
 
     def hand_on(zz):
+        all_here(xs_r.at[0, zz], xr.at[0:2, zz])
         for s, h, p in ((0, 0, pr), (1, 1, pl_)):
-            xsum(s, zz).wait_recv()
             rows = piece(p, zz)
             part[p, h, rows, :] = (
                 part[p, h, rows, :].astype(F32) + xr[s, zz].astype(F32)
@@ -159,8 +195,7 @@
             xsum(s + 4, zz).start()
 
     def root(zz):
-        for s in (2, 3, 4, 5):
-            xsum(s, zz).wait_recv()
+        all_here(xs_r.at[1, zz], xr.at[2:6, zz])
         own = piece(x, zz)
         r32[:, 0:128] = part[x, 0, own, :].astype(F32) + (
             xr[3, zz].astype(F32) + xr[4, zz].astype(F32)
@@ -173,61 +208,76 @@
                 at = SLAB * i + OWN * kk
                 frag[kk, OWN * i : OWN * (i + 1), :] = r32[at : at + OWN, :]
         for kk in range(NY):
-            ysend[zz, kk] = frag[kk].astype(BF16)
-        for o in range(1, NY):
-            kt = mod(k + o, NY)
-            rc(
-                ysend.at[zz, kt], yrecv.at[zz, k], ys_s.at[zz, o - 1], ys_r.at[zz, k], ydev[o - 1]
-            ).start()
-        yrecv[zz, k] = ysend[zz, k]
+            for h in range(2):
+                ysend[zz, kk, h] = frag[kk][:, 128 * h : 128 * h + 128].astype(BF16)
+        for n in range(6):
+            ysum_copy(zz, n).start()
+
+    def ysum_copy(zz, n):
+        row = ysend.at[zz, kof((-3, 3, 4, 4, -1, 1, -2, 2)[n])]
+        src, dst, to = [
+            (row, ymid.at[zz, 0], -1),
+            (row, ymid.at[zz, 1], 1),
+            (row.at[0], yhalf.at[zz, 0], -2),
+            (row.at[1], yhalf.at[zz, 1], 2),
+            (row, yrecv.at[zz, 0], -1),
+            (row, yrecv.at[zz, 1], 1),
+            (row, yrecv.at[zz, 2], -2),
+            (row, yrecv.at[zz, 3], 2),
+        ][n]
+        return rc(src, dst, out.at[5], ys_r.at[0 if n < 4 else 1, zz], at_y(y + NY + to))
+
+    def mid(zz):
+        all_here(ys_r.at[0, zz], ysend.at[zz, 0:3])
+        for e in range(2):
+            kk = kof((-2, 2)[e])
+            for h in range(2):
+                t = ysend[zz, kk, h].astype(F32) + ymid[zz, e, h].astype(F32)
+                if h == e:
+                    t = t + yhalf[zz, e].astype(F32)
+                ysend[zz, kk, h] = t.astype(BF16)
+            ysum_copy(zz, 6 + e).start()
 
     def zsum(zz):
-        for o in range(1, NY):
-            ks = mod(k + o, NY)
-            rc(
-                ysend.at[zz, ks], yrecv.at[zz, ks], ys_s.at[zz, o - 1], ys_r.at[zz, ks], ydev[o - 1]
-            ).wait()
-        s = yrecv[zz, 0].astype(F32)
-        for kk in range(1, NY):
-            s = s + yrecv[zz, kk].astype(F32)
-        ysum[0:48, :] = s
+        all_here(ys_r.at[1, zz], yrecv.at[zz])
+        for h in range(2):
+            t = ysend[zz, k, h].astype(F32)
+            for e in range(4):
+                t = t + yrecv[zz, e, h].astype(F32)
+            ysum[0:48, 128 * h : 128 * h + 128] = t
         for i in range(4):
             zt = 4 * zz + i
             zsend[zt] = ysum[OWN * i : OWN * i + 16, :].astype(BF16)
 
             @pl.when(zt != z)
             def _():
-                rc(zsend.at[zt], zrecv.at[z], zs_s.at[zt], zs_r.at[z], dev(x, zt, k, c)).start()
+                rc(zsend.at[zt], zrecv.at[z], out.at[6], into.at[1], dev(x, zt, k, c)).start()
 
             @pl.when(zt == z)
             def _():
                 zrecv[zt] = zsend[zt]
 
+    quarter(2).wait_recv()
+    quarter(3).wait_recv()
     term(pf)
     far(0)
+    quarter(0).wait_recv()
+    term(pl_)
+    quarter(1).wait_recv()
     term(pr)
-    term(pl_)
     near(0)
+    far(1)
     term(x)
-
-    for o in range(1, NY):
-        ks = mod(k + o, NY)
-        rc(ychunk.at[ks], ychunk.at[ks], ya_s.at[o - 1], ya_r.at[ks], ydev[o - 1]).wait()
-    for j in range(NY):
-        slab[OWN * j : OWN * (j + 1), :] = ychunk[j].astype(F32)[:OWN]
-    xslab[x] = slab[...].astype(BF16)
-    for o in range(1, NX):
-        rc(xslab.at[x], xslab.at[x], xa_s.at[o - 1], xa_r.at[x], xdev[o - 1]).start()
-    far(1)
     hand_on(0)
+    far(2)
     near(1)
-    far(2)
-    for o in range(1, NX):
-        xs = mod(x + o, NX)
-        rc(xslab.at[xs], xslab.at[xs], xa_s.at[o - 1], xa_r.at[xs], xdev[o - 1]).wait()
+
+    all_here(into.at[0], chunk.at[0 : NX * NY - 1])
     for q in range(2):
-        zpack[0:SLAB, :] = xslab[2 * q].astype(F32)[:SLAB]
-        zpack[SLAB : 2 * SLAB, :] = xslab[2 * q + 1].astype(F32)[:SLAB]
+        for e in range(2):
+            for j in range(NY):
+                at = SLAB * e + OWN * j
+                zpack[at : at + OWN, :] = chunk[(2 * q + e) * NY + j].astype(F32)[:OWN]
         for h in range(2):
             zbuf[z, q, h] = zpack[:, 128 * h : 128 * h + 128].astype(BF16)
 
@@ -240,22 +290,22 @@
     def zcopy(way, t, h):
         at = zslot(way, t - 1)
         return rc(
-            zbuf.at[at, odd, h], zbuf.at[at, odd, h], za_s.at[way, t - 1, h], za_r.at[at, h],
+            zbuf.at[at, odd, h], zbuf.at[at, odd, h], out.at[2], za_r.at[at, h],
             zright if way == 0 else zleft,
         )
 
     def zarrived(way, t, h):
         at = zslot(way, t)
         rc(
-            zbuf.at[at, odd, h], zbuf.at[at, odd, h], za_s.at[way, t - 1, h], za_r.at[at, h],
+            zbuf.at[at, odd, h], zbuf.at[at, odd, h], out.at[2], za_r.at[at, h],
             zright if way == 0 else zleft,
         ).wait_recv()
 
     def across(way, t, h, q):
         at = zslot(way, t)
         return rc(
-            zbuf.at[at, q, h], zbuf.at[at, q, h], zy_s.at[at, h], zy_r.at[at, h],
-            up if h == 0 else down,
+            zbuf.at[at, q, h], zbuf.at[at, q, h], out.at[3], zy_r.at[t - 1],
+            (up, down, right, left)[h if t < 4 else 2 + h],
         )
 
     def place(at, q, h):
@@ -278,11 +328,11 @@
                 if h in zhalves(way, t):
                     place(zslot(way, t), odd, h)
 
-    def from_y(t):
+    def from_side(t):
+        all_here(zy_r.at[t - 1], zbuf.at[0:2, 0] if t < 6 else zbuf.at[0, 0])
         for h in range(2):
             for way in range(2):
                 if h in zhalves(way, t):
-                    across(way, t, h, 1 - odd).wait_recv()
                     place(zslot(way, t), 1 - odd, h)
 
     for h in range(2):
@@ -295,54 +345,65 @@
     near(2)
     zstep(1)
     root(0)
+    hand_on(2)
     zstep(2)
-    hand_on(2)
+    mid(0)
+    root(1)
     zstep(3)
-    from_y(1)
-    root(1)
+    from_side(1)
+    zsum(0)
     zstep(4)
-    from_y(2)
-    zsum(0)
+    mid(1)
+    root(2)
+    from_side(2)
     zstep(5)
-    from_y(3)
-    root(2)
+    zsum(1)
+    mid(2)
+    from_side(3)
     zstep(6)
-    from_y(4)
-    zsum(1)
-    from_y(5)
-    from_y(6)
-    zsum(2)
-
-    def out_step(j, acc):
+    from_side(4)
+
+    def order(j):
+        return jnp.where(odd == 0, j, NCH - 1 - j)
+
+    def out_step(i, acc):
+        j = order(i)
         at = pl.multiple_of(j * CH, CH)
         w = w32[pl.ds(at, CH), :].astype(BF16)
         acc = acc + jnp.dot(tok2[:, pl.ds(at, CH)], w, preferred_element_type=F32)
         g = lax.dot_general(cot2[:, mine], w, (((1,), (1,)), ((), ())), preferred_element_type=F32)
         gi32[j] = g[:T]
         gsend[j] = g[T:].astype(BF16)
-        rc(gsend.at[j], grecv.at[j], sib_s.at[5 + j], sib_r.at[5 + j], sib).start()
+        rc(gsend.at[j], grecv.at[j], out.at[7], sib_r.at[5 + j], sib).start()
         return acc
 
-    acc = lax.fori_loop(0, NCH, out_step, jnp.zeros((2 * T, HALF), F32))
+    def join(i):
+        j = order(i)
+        rc(gsend.at[j], grecv.at[j], out.at[7], sib_r.at[5 + j], sib).wait_recv()
+        at = pl.multiple_of(j * CH, CH)
+        gi[:, pl.ds(at, CH)] = (gi32[j] + grecv[j].astype(F32)).astype(BF16)
+
+    def out_join(i, acc):
+        acc = out_step(i, acc)
+        join(i - 3)
+        return acc
+
+    acc = lax.fori_loop(0, 3, out_step, jnp.zeros((2 * T, HALF), F32))
+    zsum(2)
+    from_side(5)
+    from_side(6)
+    acc = lax.fori_loop(3, NCH, out_join, acc)
     other = pl.ds(pl.multiple_of((1 - c) * HALF, 128), HALF)
     keys[:, mine] = acc[:T].astype(BF16)
     ksend[...] = acc[T:].astype(BF16)
     ck = rc(ksend, krecv, sib_s.at[3], sib_r.at[3], sib)
     ck.start()
-
-    def join(j, _):
-        rc(gsend.at[j], grecv.at[j], sib_s.at[5 + j], sib_r.at[5 + j], sib).wait()
-        at = pl.multiple_of(j * CH, CH)
-        gi[:, pl.ds(at, CH)] = (gi32[j] + grecv[j].astype(F32)).astype(BF16)
-        return 0
-
-    lax.fori_loop(0, NCH, join, 0)
+    for i in range(NCH - 3, NCH):
+        join(i)
     ck.wait()
     keys[:, other] = krecv[...]
 
-    for o in range(1, NZ):
-        zs = mod(z + o, NZ)
-        rc(zsend.at[zs], zrecv.at[zs], zs_s.at[zs], zs_r.at[zs], zdev[o - 1]).wait()
+    all_here(into.at[1], zrecv.at[0 : NZ - 1])
     s = zrecv[0].astype(F32)
     for j in range(1, NZ):
         s = s + zrecv[j].astype(F32)
@@ -350,14 +411,14 @@
     cf = rc(fin.at[c], fin.at[c], sib_s.at[4], sib_r.at[4], sib)
     cf.start()
 
-    for t in range(1, 7):
-        for way in range(2):
-            for h in zhalves(way, t):
-                zcopy(way, t, h).wait_send()
-                across(way, t, h, odd).wait_send()
-    for s in range(6):
-        for zz in range(3):
-            xsum(s, zz).wait_send()
+    all_sent(0, tok2.at[0:T, 0:D])
+    all_sent(1, chunk.at[0 : NX * NY - 1])
+    all_sent(2, zbuf.at[0:11, 0])
+    all_sent(3, zbuf.at[0:11, 0])
+    all_sent(4, xr)
+    all_sent(5, ysend.at[:, 0:7])
+    all_sent(6, zsend.at[0 : NZ - 1])
+    all_sent(7, gsend)
     cf.wait()
     for r in range(OWN):
         rows = []
@@ -387,9 +448,7 @@
         pltpu.VMEM((2 * T, KV), BF16),
         pltpu.VMEM((2, 16, HALF), F32),
         pltpu.VMEM((16, HALF), F32),
-        pltpu.VMEM((NY, 16, HALF), BF16),
-        pltpu.VMEM((96, HALF), F32),
-        pltpu.VMEM((NX, 96, HALF), BF16),
+        pltpu.VMEM((NX * NY, 16, HALF), BF16),
         pltpu.VMEM((2 * SLAB, HALF), F32),
         pltpu.VMEM((NZ, 2, 2, 2 * SLAB, 128), BF16),
         pltpu.VMEM((ROWS, HALF), F32),
@@ -397,8 +456,10 @@
         pltpu.VMEM((6, 3, PIECE, 128), BF16),
         pltpu.VMEM((PIECE, HALF), F32),
         pltpu.VMEM((NY, 48, HALF), F32),
-        pltpu.VMEM((3, NY, 48, HALF), BF16),
-        pltpu.VMEM((3, NY, 48, HALF), BF16),
+        pltpu.VMEM((3, NY, 2, 48, 128), BF16),
+        pltpu.VMEM((3, 2, 2, 48, 128), BF16),
+        pltpu.VMEM((3, 2, 48, 128), BF16),
+        pltpu.VMEM((3, 4, 2, 48, 128), BF16),
         pltpu.VMEM((56, HALF), F32),
         pltpu.VMEM((NZ, 16, HALF), BF16),
         pltpu.VMEM((NZ, 16, HALF), BF16),
@@ -411,13 +472,9 @@
         pltpu.VMEM((OWN, HALF), BF16),
         pltpu.VMEM((1, OWN), BF16),
         dma((4,)),
-        dma((5 + NCH,)), dma((5 + NCH,)),
-        dma((NY - 1,)), dma((NY,)),
-        dma((NX - 1,)), dma((NX,)),
-        dma((2, 6, 2)), dma((NZ, 2)), dma((NZ, 2)), dma((NZ, 2)),
-        dma((6, 3)), dma((6, 3)),
-        dma((3, NY - 1)), dma((3, NY)),
-        dma((NZ,)), dma((NZ,)),
+        dma((5,)), dma((5 + NCH,)),
+        dma((8,)), dma((2,)), dma((NX,)),
+        dma((NZ, 2)), dma((6,)), dma((2, 3)), dma((2, 3)),
     ]
     vmem = pl.BlockSpec(memory_space=pltpu.VMEM)
     hbm = pl.BlockSpec(memory_space=pl.ANY)

time: 69.7 us -> 64 us (0.918)
  Pallas kernels: 68.9 us -> 63.2 us
    pallas_call x1, Pallas kernels: 67.9 us -> 62.2 us  [per_device(): pl.pallas_call(functools.partial(kernel, 1.0 / total ** 0.5), out_shape=(...]
where the time goes in v3:
time: 64 us; the launch traced here: 63.8 us
  Pallas kernels  63.2 us (99%)
  between operations  0.64 us (1%)
    pallas_call x1, Pallas kernels, per_device(): pl.pallas_call(functools.partial(kernel, 1.0 / total ** 0.5), out_shape=(...  62.2 us

profile of v3, /device:TPU:1, one launch (start us, length us, event | category | flops | bytes accessed | tf_op | source)
XLA Modules:
  0.0 63.8 jit_solution(13441849741976346715)
XLA Ops:
  0.6 62.2 %fused.1 = (bf16[128,512]{1,0:T(8,128)(2,1)S(1)}, bf16[128,4096]{1,0:T(8,128)(2,1)S(1)}, f32[11,256]{1,0:T(8,128)S(1)}) custom-call(bf16[128,4096]{1,0:T(8,128)(2,1)} %tok_hbm.1, bf16[128,512]{1,0:T(8,128)(2,1)} %cot_hbm.1, bf16[11,256]{1,0:T(8,128)(2,1)} %codes_hbm.1, bf16[1,11]{1,0:T(2,128)(2,1)} %bitcast.1), custom_call_target="tpu_custom_call" | custom-call | tf_op jit(solution)/shard_map/fused/pallas_call | solution.py:482
  62.8 1.0 %store.1 = (bf16[128,512]{1,0:T(8,128)(2,1)}, bf16[128,4096]{1,0:T(8,128)(2,1)}, f32[11,256]{1,0:T(8,128)}) custom-call(bf16[128,512]{1,0:T(8,128)(2,1)S(1)} %get-tuple-element.6.keys, bf16[128,4096]{1,0:T(8,128)(2,1)S(1)} %get-tuple-element.7.gi, f32[11,256]{1,0:T(8,128)S(1)} %get-tuple-element.8.gw), custom_call_target="tpu_custom_call" | custom-call | tf_op jit(solution)/shard_map/store/pallas_call | solution.py:497

commit v4 on v3

--- a/solution.py
+++ b/solution.py
@@ -341,25 +341,25 @@
     for q in range(2):
         for h in range(2):
             place(z, q, h)
+    zstep(1)
     hand_on(1)
     near(2)
-    zstep(1)
     root(0)
+    zstep(2)
     hand_on(2)
-    zstep(2)
+    zstep(3)
     mid(0)
     root(1)
-    zstep(3)
+    zstep(4)
     from_side(1)
     zsum(0)
-    zstep(4)
+    root(2)
     mid(1)
-    root(2)
+    zstep(5)
     from_side(2)
-    zstep(5)
+    from_side(3)
+    mid(2)
     zsum(1)
-    mid(2)
-    from_side(3)
     zstep(6)
     from_side(4)
 
@@ -383,22 +383,17 @@
         at = pl.multiple_of(j * CH, CH)
         gi[:, pl.ds(at, CH)] = (gi32[j] + grecv[j].astype(F32)).astype(BF16)
 
-    def out_join(i, acc):
-        acc = out_step(i, acc)
-        join(i - 3)
-        return acc
-
     acc = lax.fori_loop(0, 3, out_step, jnp.zeros((2 * T, HALF), F32))
+    from_side(5)
     zsum(2)
-    from_side(5)
     from_side(6)
-    acc = lax.fori_loop(3, NCH, out_join, acc)
+    acc = lax.fori_loop(3, NCH, out_step, acc)
     other = pl.ds(pl.multiple_of((1 - c) * HALF, 128), HALF)
     keys[:, mine] = acc[:T].astype(BF16)
     ksend[...] = acc[T:].astype(BF16)
     ck = rc(ksend, krecv, sib_s.at[3], sib_r.at[3], sib)
     ck.start()
-    for i in range(NCH - 3, NCH):
+    for i in range(NCH):
         join(i)
     ck.wait()
     keys[:, other] = krecv[...]

time: 64 us -> 62.9 us (0.983)
  Pallas kernels: 63.2 us -> 62.2 us
    pallas_call x1, Pallas kernels: 62.2 us -> 61.1 us  [per_device(): pl.pallas_call(functools.partial(kernel, 1.0 / total ** 0.5), out_shape=(...]
where the time goes in v4:
time: 62.9 us; the launch traced here: 62.8 us
  Pallas kernels  62.2 us (99%)
  between operations  0.64 us (1%)
    pallas_call x1, Pallas kernels, per_device(): pl.pallas_call(functools.partial(kernel, 1.0 / total ** 0.5), out_shape=(...  61.1 us

profile of v4, /device:TPU:1, one launch (start us, length us, event | category | flops | bytes accessed | tf_op | source)
XLA Modules:
  0.0 62.8 jit_solution(5042258289869817855)
XLA Ops:
  0.6 61.1 %fused.1 = (bf16[128,512]{1,0:T(8,128)(2,1)S(1)}, bf16[128,4096]{1,0:T(8,128)(2,1)S(1)}, f32[11,256]{1,0:T(8,128)S(1)}) custom-call(bf16[128,4096]{1,0:T(8,128)(2,1)} %tok_hbm.1, bf16[128,512]{1,0:T(8,128)(2,1)} %cot_hbm.1, bf16[11,256]{1,0:T(8,128)(2,1)} %codes_hbm.1, bf16[1,11]{1,0:T(2,128)(2,1)} %bitcast.1), custom_call_target="tpu_custom_call" | custom-call | tf_op jit(solution)/shard_map/fused/pallas_call | solution.py:477
  61.8 1.0 %store.1 = (bf16[128,512]{1,0:T(8,128)(2,1)}, bf16[128,4096]{1,0:T(8,128)(2,1)}, f32[11,256]{1,0:T(8,128)}) custom-call(bf16[128,512]{1,0:T(8,128)(2,1)S(1)} %get-tuple-element.6.keys, bf16[128,4096]{1,0:T(8,128)(2,1)S(1)} %get-tuple-element.7.gi, f32[11,256]{1,0:T(8,128)S(1)} %get-tuple-element.8.gw), custom_call_target="tpu_custom_call" | custom-call | tf_op jit(solution)/shard_map/store/pallas_call | solution.py:492

commit v5 on v4

--- a/solution.py
+++ b/solution.py
@@ -210,7 +210,11 @@
         for kk in range(NY):
             for h in range(2):
                 ysend[zz, kk, h] = frag[kk][:, 128 * h : 128 * h + 128].astype(BF16)
-        for n in range(6):
+        for n in range(4):
+            ysum_copy(zz, n).start()
+
+    def direct(zz):
+        for n in (4, 5):
             ysum_copy(zz, n).start()
 
     def ysum_copy(zz, n):
@@ -346,16 +350,19 @@
     near(2)
     root(0)
     zstep(2)
+    direct(0)
     hand_on(2)
     zstep(3)
     mid(0)
     root(1)
     zstep(4)
+    direct(1)
     from_side(1)
     zsum(0)
     root(2)
     mid(1)
     zstep(5)
+    direct(2)
     from_side(2)
     from_side(3)
     mid(2)
@@ -383,11 +390,11 @@
         at = pl.multiple_of(j * CH, CH)
         gi[:, pl.ds(at, CH)] = (gi32[j] + grecv[j].astype(F32)).astype(BF16)
 
-    acc = lax.fori_loop(0, 3, out_step, jnp.zeros((2 * T, HALF), F32))
+    acc = lax.fori_loop(0, 3, out_step, jnp.zeros((2 * T, HALF), F32), unroll=True)
     from_side(5)
     zsum(2)
     from_side(6)
-    acc = lax.fori_loop(3, NCH, out_step, acc)
+    acc = lax.fori_loop(3, NCH, out_step, acc, unroll=True)
     other = pl.ds(pl.multiple_of((1 - c) * HALF, 128), HALF)
     keys[:, mine] = acc[:T].astype(BF16)
     ksend[...] = acc[T:].astype(BF16)
@@ -395,8 +402,6 @@
     ck.start()
     for i in range(NCH):
         join(i)
-    ck.wait()
-    keys[:, other] = krecv[...]
 
     all_here(into.at[1], zrecv.at[0 : NZ - 1])
     s = zrecv[0].astype(F32)
@@ -405,6 +410,8 @@
     fin[c] = s
     cf = rc(fin.at[c], fin.at[c], sib_s.at[4], sib_r.at[4], sib)
     cf.start()
+    ck.wait()
+    keys[:, other] = krecv[...]
 
     all_sent(0, tok2.at[0:T, 0:D])
     all_sent(1, chunk.at[0 : NX * NY - 1])

time: 62.9 us -> 62.7 us (level)
  no operation moved by 1% of the time
where the time goes in v5:
time: 62.7 us; the launch traced here: 62.6 us
  Pallas kernels  61.9 us (99%)
  between operations  0.64 us (1%)
    pallas_call x1, Pallas kernels, per_device(): pl.pallas_call(functools.partial(kernel, 1.0 / total ** 0.5), out_shape=(...  60.9 us

profile of v5, /device:TPU:1, one launch (start us, length us, event | category | flops | bytes accessed | tf_op | source)
XLA Modules:
  0.0 62.6 jit_solution(14388443238589345200)
XLA Ops:
  0.6 60.9 %fused.1 = (bf16[128,512]{1,0:T(8,128)(2,1)S(1)}, bf16[128,4096]{1,0:T(8,128)(2,1)S(1)}, f32[11,256]{1,0:T(8,128)S(1)}) custom-call(bf16[128,4096]{1,0:T(8,128)(2,1)} %tok_hbm.1, bf16[128,512]{1,0:T(8,128)(2,1)} %cot_hbm.1, bf16[11,256]{1,0:T(8,128)(2,1)} %codes_hbm.1, bf16[1,11]{1,0:T(2,128)(2,1)} %bitcast.1), custom_call_target="tpu_custom_call" | custom-call | tf_op jit(solution)/shard_map/fused/pallas_call | solution.py:484
  61.6 1.0 %store.1 = (bf16[128,512]{1,0:T(8,128)(2,1)}, bf16[128,4096]{1,0:T(8,128)(2,1)}, f32[11,256]{1,0:T(8,128)}) custom-call(bf16[128,512]{1,0:T(8,128)(2,1)S(1)} %get-tuple-element.6.keys, bf16[128,4096]{1,0:T(8,128)(2,1)S(1)} %get-tuple-element.7.gi, f32[11,256]{1,0:T(8,128)S(1)} %get-tuple-element.8.gw), custom_call_target="tpu_custom_call" | custom-call | tf_op jit(solution)/shard_map/store/pallas_call | solution.py:499
